TPU v7x, 32 devices: a whole 2x2x4 slice. The times are simulated.
32 devices in a mesh: grp: 4 (over x, core), tile: 8 (over z, y).
Axes of the slice: x: 2, y: 2, z: 4, core: 2. Of those that a mesh axis runs over, the one named last changes fastest.
Arguments:
- tx_fields: bfloat16 [64, 8192], P(None, 'tile'), may hold values from -6 to 6
- rx_fields: bfloat16 [128, 8192], P(None, 'tile'), may hold values from -6 to 6
- layer_of_cell: int32 [8192], P('tile'), may hold values from 0 to 31
- layer_cond: float32 [32], replicated, may hold values from 0.05 to 5
- tx_of_row: int32 [1408], replicated, may hold values from 0 to 63
- rx_of_row: int32 [1408], replicated, may hold values from 0 to 127
- damping: float32 [1408], replicated, may hold values from 0.5 to 5
- panel_order: int32 [1408], replicated, may hold values from 0 to 1407, each once
Outputs:
- trailing: float32 [1408, 1408], P('grp', 'tile')
- factor: float32 [1408, 1024], P('grp')
Inputs may be any that keep to these rules, and one draw needn't show every extreme that they name: `panel_order`: each data row appears exactly once; panel k is entries k * 512 to (k + 1) * 512 - 1.
All inputs are finite; a program needn't handle non-finite values.
Results may differ from a plain program's by a relative error of at most 0.0014.
Values may be sent and summed in bfloat16 or wider, within the bound.
No kernel may reach another device: no remote copies, remote signals or barrier semaphores. Data moves between devices by JAX's collectives and lax.ppermute only.
A program may use at most 64 MiB of HBM per device.

v0:
```python
import jax
import jax.numpy as jnp
from jax import lax
from jax.sharding import PartitionSpec as P

PANEL = 512
NPAN = 2


highest = lax.Precision.HIGHEST


def shards(
    tx_fields, rx_fields, layer_of_cell, layer_cond, tx_of_row, rx_of_row, damping, panel_order
):
    grp_count = lax.axis_size("grp")
    tile_count = lax.axis_size("tile")
    tile_cells = tx_fields.shape[1]
    total_rows = tx_of_row.shape[0]
    group_rows = total_rows // grp_count
    tile_cols = total_rows // tile_count
    group_start = lax.axis_index("grp") * group_rows
    tile_start = lax.axis_index("tile") * tile_cols
    levels = jnp.arange(layer_cond.shape[0], dtype=jnp.int32)
    layer_hot = (levels[:, None] == layer_of_cell[None, :]).astype(jnp.float32)
    cell_cond = jnp.dot(layer_cond[None, :], layer_hot, precision=highest)[0]
    contract = (((1,), (1,)), ((), ()))
    product = (
        jnp.take(
            tx_fields, lax.dynamic_slice_in_dim(tx_of_row, group_start, group_rows), axis=0
        ).astype(jnp.float32)
        * jnp.take(
            rx_fields, lax.dynamic_slice_in_dim(rx_of_row, group_start, group_rows), axis=0
        ).astype(jnp.float32)
        * cell_cond[None, :]
    )
    sens_own = product.astype(jnp.bfloat16)
    block_cols = lax.psum_scatter(
        lax.dot_general(
            lax.all_gather(sens_own, "grp", axis=0, tiled=True),
            sens_own,
            contract,
            preferred_element_type=jnp.float32,
        ),
        "tile",
        scatter_dimension=0,
        tiled=True,
    )
    cell_total = tile_cells * tile_count
    row_ids = group_start + jnp.arange(group_rows, dtype=jnp.int32)
    col_ids = tile_start + jnp.arange(tile_cols, dtype=jnp.int32)
    on_diagonal = row_ids[:, None] == col_ids[None, :]
    damp_rows = lax.dynamic_slice_in_dim(damping, group_start, group_rows)
    trailing = block_cols.T / cell_total + jnp.where(on_diagonal, damp_rows[:, None], 0.0)
    factor_parts = []
    for turn_index in range(NPAN):
        chosen = panel_order[turn_index * PANEL : (turn_index + 1) * PANEL]
        col_pick = (col_ids[:, None] == chosen[None, :]).astype(jnp.float32)
        row_pick = (chosen[:, None] == row_ids[None, :]).astype(jnp.float32)
        panel_strip = lax.psum(jnp.dot(row_pick, trailing, precision=highest), "grp")
        columns, diag_block = lax.psum(
            (
                jnp.dot(trailing, col_pick, precision=highest),
                jnp.dot(panel_strip, col_pick, precision=highest),
            ),
            "tile",
        )
        block_factor = jnp.linalg.cholesky(diag_block)
        panel_factor = lax.linalg.triangular_solve(
            block_factor, columns, left_side=False, lower=True, transpose_a=True
        )
        column_factor = lax.linalg.triangular_solve(
            block_factor, panel_strip.T, left_side=False, lower=True, transpose_a=True
        )
        trailing = trailing - jnp.dot(panel_factor, column_factor.T, precision=highest)
        factor_parts.append(panel_factor)
    return (trailing, jnp.concatenate(factor_parts, axis=1))


def solution(mesh):
    placed = (P(None, "tile"), P(None, "tile"), P("tile"), P(), P(), P(), P(), P())
    return jax.shard_map(
        shards,
        mesh=mesh,
        in_specs=placed,
        out_specs=(P("grp", "tile"), P("grp", None)),
        check_vma=False,
    )
```

profile of v0, /device:TPU:0, one launch (start us, length us, event | category | flops | bytes accessed | tf_op | source)
XLA Modules:
  0.0 677.9 jit_solution(9557811862079232964)
XLA Ops:
  7.2 0.8 compare_and_fusion
  8.1 3.7 gather_fusion
  11.9 2.1 gather_fusion.1
  14.2 1.2 multiply_convert_fusion
  15.5 29.8 %all-gather.2.cloned.1.call-done = bf16[1408,1024]{1,0:T(8,128)(2,1)} async-done(((bf16[352,1024]{1,0:T(8,128)(2,1)}), bf16[1408,1024]{1,0:T(8,128)(2,1)}) %all-gather.2.cloned.1.call-update) | async-done | bytes 2883600 | tf_op jit(solution)/shard_map/all_gather | solution.py:40
  45.3 5.0 fusion.170
  50.4 0.8 dynamic_slice.11
  51.2 67.5 %reduce-scatter.2.cloned.1.call-done = f32[176,352]{1,0:T(8,128)} async-done(((f32[1408,352]{1,0:T(8,128)}), f32[176,352]{1,0:T(8,128)}) %reduce-scatter.2.cloned.1.call-update) | async-done | bytes 247824 | tf_op jit(solution)/shard_map/reduce_scatter | solution.py:38
  118.8 2.4 fusion.4
  121.2 2.5 fusion.34
  123.7 29.6 %all-reduce.8.cloned.1.call-done = f32[512,176]{0,1:T(8,128)} async-done(((f32[512,176]{0,1:T(8,128)}), f32[512,176]{0,1:T(8,128)}) %all-reduce.8.cloned.1.call-update) | async-done | bytes 360464 | tf_op jit(solution)/shard_map/psum | solution.py:60
  153.2 2.7 fusion.36
  156.2 94.9 %all-reduce.14.cloned.1.call-done = (f32[352,512]{1,0:T(8,128)}, f32[512,512]{0,1:T(8,128)}) async-done(((f32[352,512]{1,0:T(8,128)}, f32[512,512]{0,1:T(8,128)}), (f32[352,512]{1,0:T(8,128)}, f32[512,512]{0,1:T(8,128)})) %all-reduce.14.cloned.1.call-update) | async-done | bytes 1769488 | tf_op jit(solution)/shard_map/psum | solution.py:61
  251.1 1.6 copy.11
  253.1 11.7 %cholesky.286 = f32[128,128]{1,0:T(8,128)S(1)} custom-call(f32[128,128]{1,0:T(8,128)S(1)} %cholesky.426), custom_call_target="Cholesky" | custom-call | tf_op jit(solution)/shard_map/jit(cholesky)/cholesky | solution.py:68
  264.9 9.8 %custom-call.31 = f32[1,128,128]{1,2,0:T(8,128)S(1)} custom-call(f32[1,128,128]{2,1,0:T(8,128)S(1)} %get-tuple-element.84), custom_call_target="InvertDiagBlocksLowerTriangular" | custom-call | tf_op jit(solution)/shard_map/jit(cholesky)/cholesky | solution.py:68
  275.4 11.7 %cholesky.305 = f32[128,128]{1,0:T(8,128)S(1)} custom-call(f32[128,128]{1,0:T(8,128)S(1)} %cholesky.430), custom_call_target="Cholesky" | custom-call | tf_op jit(solution)/shard_map/jit(cholesky)/cholesky | solution.py:68
  287.2 0.7 compare_reduce_fusion.6
  287.8 0.6 compare_reduce_fusion.7
  288.5 10.0 %custom-call.32 = f32[1,128,128]{1,2,0:T(8,128)S(1)} custom-call(f32[1,128,128]{2,1,0:T(8,128)S(1)} %get-tuple-element.81), custom_call_target="InvertDiagBlocksLowerTriangular" | custom-call | tf_op jit(solution)/shard_map/jit(cholesky)/cholesky | solution.py:68
  299.1 11.7 %cholesky.326 = f32[128,128]{1,0:T(8,128)S(1)} custom-call(f32[128,128]{1,0:T(8,128)S(1)} %cholesky.435), custom_call_target="Cholesky" | custom-call | tf_op jit(solution)/shard_map/jit(cholesky)/cholesky | solution.py:68
  310.9 0.7 compare_reduce_fusion.5
  311.5 9.8 %custom-call.33 = f32[1,128,128]{1,2,0:T(8,128)S(1)} custom-call(f32[1,128,128]{2,1,0:T(8,128)S(1)} %get-tuple-element.78), custom_call_target="InvertDiagBlocksLowerTriangular" | custom-call | tf_op jit(solution)/shard_map/jit(cholesky)/cholesky | solution.py:68
  322.0 11.7 %cholesky.343 = f32[128,128]{1,0:T(8,128)S(1)} custom-call(f32[128,128]{1,0:T(8,128)S(1)} %convolution_subtract_fusion.19), custom_call_target="Cholesky" | custom-call | tf_op jit(solution)/shard_map/jit(cholesky)/cholesky | solution.py:68
  333.7 0.7 compare_reduce_fusion.4
  337.6 8.1 %while.8 = (s32[]{:T(128)}, f32[512,512]{1,0:T(8,128)S(1)}, s32[4,2]{0,1:T(2,128)S(1)}, f32[4,128,128]{2,1,0:T(8,128)S(1)}, s32[]{:T(128)}) while((s32[]{:T(128)}, f32[512,512]{1,0:T(8,128)S(1)}, s32[4,2]{0,1:T(2,128)S(1)}, f32[4,128,128]{2,1,0:T(8,128)S(1)}, s32[]{:T(128)}) %tuple.67), condition=%wide.while_cond, body=%wide.while_body.sunk | while | flops 2 | bytes 131181 | solution.py:69
  338.2 1.4 bitcast_dynamic-update-slice_fusion.4
  340.3 1.4 bitcast_dynamic-update-slice_fusion.4
  342.3 1.4 bitcast_dynamic-update-slice_fusion.4
  344.3 1.4 bitcast_dynamic-update-slice_fusion.4
  345.7 39.3 %custom-call.34 = f32[4,128,128]{1,2,0:T(8,128)S(1)} custom-call(f32[4,128,128]{2,1,0:T(8,128)S(1)} %get-tuple-element.33), custom_call_target="InvertDiagBlocksLowerTriangular" | custom-call | tf_op jit(solution)/shard_map/triangular_solve/custom-call.3 | solution.py:69
  389.6 0.9 convolution_subtract_fusion.1
  390.5 1.4 fusion.2
  392.2 1.5 fusion.30
  393.7 30.4 %all-reduce.10.cloned.1.call-done = f32[512,176]{0,1:T(8,128)} async-done(((f32[512,176]{0,1:T(8,128)}), f32[512,176]{0,1:T(8,128)}) %all-reduce.10.cloned.1.call-update) | async-done | bytes 360464 | tf_op jit(solution)/shard_map/psum | solution.py:60
  424.1 2.7 fusion.32
  426.9 95.6 %all-reduce.12.cloned.1.call-done = (f32[352,512]{1,0:T(8,128)}, f32[512,512]{0,1:T(8,128)}) async-done(((f32[352,512]{1,0:T(8,128)}, f32[512,512]{0,1:T(8,128)}), (f32[352,512]{1,0:T(8,128)}, f32[512,512]{0,1:T(8,128)})) %all-reduce.12.cloned.1.call-update) | async-done | bytes 1769488 | tf_op jit(solution)/shard_map/psum | solution.py:61
  522.5 1.6 copy.13
  524.4 1.0 copy-done.3
  525.4 11.7 %cholesky.358 = f32[128,128]{1,0:T(8,128)S(1)} custom-call(f32[128,128]{1,0:T(8,128)S(1)} %cholesky.439), custom_call_target="Cholesky" | custom-call | tf_op jit(solution)/shard_map/jit(cholesky)/cholesky | solution.py:68
  537.3 9.8 %custom-call.36 = f32[1,128,128]{1,2,0:T(8,128)S(1)} custom-call(f32[1,128,128]{2,1,0:T(8,128)S(1)} %get-tuple-element.74), custom_call_target="InvertDiagBlocksLowerTriangular" | custom-call | tf_op jit(solution)/shard_map/jit(cholesky)/cholesky | solution.py:68
  547.1 1.2 constant_dynamic-update-slice_fusion.3
  548.3 1.3 convolution_subtract_fusion.2
  549.6 11.9 %cholesky.377 = f32[128,128]{1,0:T(8,128)S(1)} custom-call(f32[128,128]{1,0:T(8,128)S(1)} %cholesky.443), custom_call_target="Cholesky" | custom-call | tf_op jit(solution)/shard_map/jit(cholesky)/cholesky | solution.py:68
  561.5 0.7 compare_reduce_fusion.2
  562.2 0.7 compare_reduce_fusion.3
  562.9 9.8 %custom-call.37 = f32[1,128,128]{1,2,0:T(8,128)S(1)} custom-call(f32[1,128,128]{2,1,0:T(8,128)S(1)} %get-tuple-element.71), custom_call_target="InvertDiagBlocksLowerTriangular" | custom-call | tf_op jit(solution)/shard_map/jit(cholesky)/cholesky | solution.py:68
  573.0 1.3 convolution_subtract_fusion.10
  574.3 11.7 %cholesky.398 = f32[128,128]{1,0:T(8,128)S(1)} custom-call(f32[128,128]{1,0:T(8,128)S(1)} %cholesky.448), custom_call_target="Cholesky" | custom-call | tf_op jit(solution)/shard_map/jit(cholesky)/cholesky | solution.py:68
  586.0 0.7 compare_reduce_fusion.1
  586.7 9.8 %custom-call.38 = f32[1,128,128]{1,2,0:T(8,128)S(1)} custom-call(f32[1,128,128]{2,1,0:T(8,128)S(1)} %get-tuple-element.68), custom_call_target="InvertDiagBlocksLowerTriangular" | custom-call | tf_op jit(solution)/shard_map/jit(cholesky)/cholesky | solution.py:68
  596.8 1.2 convolution_subtract_fusion.18
  598.0 11.9 %cholesky.415 = f32[128,128]{1,0:T(8,128)S(1)} custom-call(f32[128,128]{1,0:T(8,128)S(1)} %convolution_subtract_fusion.18), custom_call_target="Cholesky" | custom-call | tf_op jit(solution)/shard_map/jit(cholesky)/cholesky | solution.py:68
  610.0 0.6 compare_reduce_fusion
  613.4 8.1 %while.9 = (s32[]{:T(128)}, f32[512,512]{1,0:T(8,128)S(1)}, s32[4,2]{0,1:T(2,128)S(1)}, f32[4,128,128]{2,1,0:T(8,128)S(1)}, s32[]{:T(128)}) while((s32[]{:T(128)}, f32[512,512]{1,0:T(8,128)S(1)}, s32[4,2]{0,1:T(2,128)S(1)}, f32[4,128,128]{2,1,0:T(8,128)S(1)}, s32[]{:T(128)}) %tuple.87), condition=%wide.while_cond.clone, body=%wide.while_body.clone.sunk | while | flops 2 | bytes 131181 | solution.py:69
  614.0 1.4 bitcast_dynamic-update-slice_fusion.5
  616.0 1.4 bitcast_dynamic-update-slice_fusion.5
  618.0 1.4 bitcast_dynamic-update-slice_fusion.5
  620.0 1.4 bitcast_dynamic-update-slice_fusion.5
  621.4 0.7 copy-done.9
  622.1 40.1 %custom-call.39 = f32[4,128,128]{1,2,0:T(8,128)S(1)} custom-call(f32[4,128,128]{2,1,0:T(8,128)} %copy-done.9), custom_call_target="InvertDiagBlocksLowerTriangular" | custom-call | tf_op jit(solution)/shard_map/triangular_solve/custom-call.3 | solution.py:69
  662.3 1.2 fusion.84
  665.8 1.2 maximum_maximum_fusion
  669.0 1.6 convolution_subtract_fusion
  (117 shorter events, 18.6 us)
Async XLA Ops:
  7.2 4.7 copy-start
  7.2 38.1 %all-gather.2.cloned.1.call-start = ((), (), s32[]{:S(2)}) async-start(), calls=%async_computation.1 | async-start | bytes 3604480 | tf_op jit(solution)/shard_map/all_gather | solution.py:40
  11.8 2.1 copy-start.11
  11.8 2.1 copy-start.12
  15.4 103.3 %reduce-scatter.2.cloned.1.call-start = ((), (), s32[]{:S(2)}) async-start(), calls=%async_computation.2 | async-start | bytes 2433024 | tf_op jit(solution)/shard_map/reduce_scatter | solution.py:38
  50.4 0.9 copy-start.10
  50.4 102.8 %all-reduce.8.cloned.1.call-start = ((), (), s32[]{:S(2)}) async-start(), calls=%async_computation.3 | async-start | bytes 720896 | tf_op jit(solution)/shard_map/psum | solution.py:60
  121.2 130.0 %all-reduce.14.cloned.1.call-start = ((), (), s32[]{:S(2)}) async-start(), calls=%async_computation.6 | async-start | bytes 3538944 | tf_op jit(solution)/shard_map/psum | solution.py:61
  156.0 268.2 %all-reduce.10.cloned.1.call-start = ((), (), s32[]{:S(2)}) async-start(), calls=%async_computation.4 | async-start | bytes 720896 | tf_op jit(solution)/shard_map/psum | solution.py:60
  251.1 1.7 copy-start.1
  337.0 48.0 %copy-start.5 = (f32[512,176]{0,1:T(8,128)S(1)}, f32[512,176]{0,1:T(8,128)}, u32[]{:S(2)}) copy-start(f32[512,176]{0,1:T(8,128)} %all-reduce.8.cloned.1.call-done) | copy-start | bytes 1081348
  337.6 49.4 %copy-start.6 = (f32[352,512]{1,0:T(8,128)S(1)}, f32[352,512]{1,0:T(8,128)}, u32[]{:S(2)}) copy-start(f32[352,512]{1,0:T(8,128)} %get-tuple-element.55) | copy-start | bytes 2162692
  387.9 1.7 copy-start.8
  392.0 130.5 %all-reduce.12.cloned.1.call-start = ((), (), s32[]{:S(2)}) async-start(), calls=%async_computation.5 | async-start | bytes 3538944 | tf_op jit(solution)/shard_map/psum | solution.py:61
  522.5 1.7 copy-start.2
  524.4 1.0 copy-start.3
  613.3 50.2 %copy-start.7 = (f32[352,512]{1,0:T(8,128)S(1)}, f32[352,512]{1,0:T(8,128)}, u32[]{:S(2)}) copy-start(f32[352,512]{1,0:T(8,128)} %get-tuple-element.53) | copy-start | bytes 2162692
  621.4 0.7 copy-start.9
  665.8 1.2 copy-start.4
Sparse Core Ops, SparseCore 0:
  15.6 29.7 all-gather.1
  50.5 68.2 reduce-scatter.1
  121.7 31.5 all-reduce.7
  157.2 93.8 all-reduce.13
  392.1 31.9 all-reduce.9
  428.6 93.8 all-reduce.11
where the time goes:
time: 683 us; the launch traced here: 678 us
  waiting for transfers between devices  348 us (51%)
  other arithmetic  243 us (36%)
  matrix products  38.1 us (6%)
  local copies, waits for them, and re-layouts  27.9 us (4%)
  between operations  20.4 us (3%)
    psum x2, waiting for transfers between devices, shards(): lax.psum((jnp.dot(trailing, col_pick, precision=highest), jnp.dot(panel_s...  191 us
    another operation x30, other arithmetic, shards(): block_factor = jnp.linalg.cholesky(diag_block)  159 us
    another operation x5, other arithmetic, shards(): lax.linalg.triangular_solve(block_factor, columns, left_side=False, lower...  80.1 us
    reduce_scatter x1, waiting for transfers between devices, shards(): lax.psum_scatter(lax.dot_general(lax.all_gather(sens_own, 'grp', axis=0,...  67.5 us
    psum x2, waiting for transfers between devices, shards(): lax.psum(jnp.dot(row_pick, trailing, precision=highest), 'grp')  60 us
    all_gather x1, waiting for transfers between devices, shards(): lax.all_gather(sens_own, 'grp', axis=0, tiled=True)  29.8 us
    another operation x27, local copies, waits for them, and re-layouts, shards(): lax.linalg.triangular_solve(block_factor, columns, left_side=False, lower...  16 us
  transfers between devices with their start and end apart: 6, of which 6 were waited for; matrix products, arithmetic and copies ran while one was open for 1% of the time, Pallas kernels for 0%

commit v1 on v0

v1 whole, which is shorter than its diff:
```python
import functools

import jax
import jax.numpy as jnp
from jax import lax
from jax.experimental import pallas as pl
from jax.experimental.pallas import tpu as pltpu
from jax.sharding import PartitionSpec as P

PANEL = 512
NPAN = 2
BLOCK = 128
STEP = 16
CHUNK = 512
PAD = 16


def halves(value):
    high = value.astype(jnp.bfloat16)
    low = (value - high.astype(jnp.float32)).astype(jnp.bfloat16)
    return high, low


def product(left, right, dims):
    def dot(a, b):
        return lax.dot_general(a, b, (dims, ((), ())), preferred_element_type=jnp.float32)

    return dot(left[0], right[0]) + (dot(left[0], right[1]) + dot(left[1], right[0]))


ROWS_ROWS = ((1,), (1,))
PLAIN = ((1,), (0,))


def factor_block(block, work, upper):
    size = block.shape[0]
    row = lax.broadcasted_iota(jnp.int32, (size, size), 0)
    col = lax.broadcasted_iota(jnp.int32, (size, size), 1)
    eye = (row == col).astype(jnp.float32)
    work[:, :size] = block
    work[:, size:] = eye
    sub = lax.broadcasted_iota(jnp.int32, (STEP, size), 0)
    wide = (STEP, size)
    rows0, rows1 = block[:STEP, :], eye[:STEP, :]
    for at in range(0, size, STEP):
        cols = [jnp.broadcast_to(rows0[:, at + k : at + k + 1], wide) for k in range(STEP)]
        more = at + STEP < size
        if more:
            after = work[at + STEP : at + 2 * STEP, :]
            after_cols = [jnp.broadcast_to(after[:, at + k : at + k + 1], wide) for k in range(STEP)]
        done0 = done1 = jnp.zeros(wide, jnp.float32)
        for j in range(STEP):
            pivot = jnp.broadcast_to(cols[j][j : j + 1, :], wide)
            ratio = (cols[j] - jnp.where(sub == j, 1.0, 0.0)) * (1.0 / pivot)
            root = lax.rsqrt(pivot)
            row0 = jnp.broadcast_to(rows0[j : j + 1, :], wide)
            row1 = jnp.broadcast_to(rows1[j : j + 1, :], wide)
            done0 = jnp.where(sub == j, row0 * root, done0)
            done1 = jnp.where(sub == j, row1 * root, done1)
            rows0 = rows0 - ratio * row0
            rows1 = rows1 - ratio * row1
            for k in range(j + 1, STEP):
                cols[k] = cols[k] - ratio * jnp.broadcast_to(cols[k][j : j + 1, :], wide)
        upper[at : at + STEP, :size] = done0
        upper[at : at + STEP, size:] = done1
        if not more:
            break
        terms0 = [after_cols[k] * jnp.broadcast_to(rows0[k : k + 1, :], wide) for k in range(STEP)]
        terms1 = [after_cols[k] * jnp.broadcast_to(rows1[k : k + 1, :], wide) for k in range(STEP)]
        while len(terms0) > 1:
            terms0 = [a + b for a, b in zip(terms0[::2], terms0[1::2])]
            terms1 = [a + b for a, b in zip(terms1[::2], terms1[1::2])]
        if at + 2 * STEP < size:
            solved = jnp.concatenate([rows0, rows1], axis=1)
            parts = [solved, jnp.zeros((size - at - STEP, 2 * size), jnp.float32)]
            if at > 0:
                parts.insert(0, jnp.zeros((at, 2 * size), jnp.float32))
            rest = work[at + 2 * STEP :, :]
            work[at + 2 * STEP :, :] = rest - product(
                halves(rest[:, :size]), halves(jnp.concatenate(parts, axis=0)), PLAIN
            )
        rows0 = after[:, :size] - terms0[0]
        rows1 = after[:, size:] - terms1[0]


def body(
    chosen_cols,
    cell_total,
    place,
    cells,
    hot,
    layer_cond,
    damping,
    order,
    trailing,
    factor,
    gram,
    sens,
    high,
    low,
    column,
    work,
    upper,
):
    rows = gram.shape[0]
    chunk = pl.program_id(0)
    ntx, nrx = hot.shape[1] - layer_cond.shape[1], layer_cond.shape[1]
    strips = [(a, min(a + 2 * BLOCK, rows)) for a in range(0, rows, 2 * BLOCK)]

    @pl.when(chunk == 0)
    def _():
        gram[...] = jnp.zeros_like(gram)

    nlayer = layer_cond.shape[0]
    layer = cells[0, ntx + nrx : ntx + nrx + 1, :].astype(jnp.float32)
    level = lax.broadcasted_iota(jnp.int32, (nlayer, layer.shape[1]), 0).astype(jnp.float32)
    cond = jnp.sum(jnp.where(level == layer, layer_cond[:, :1], 0.0), axis=0, keepdims=True)
    for a, b in strips:
        tx = jnp.dot(hot[a:b, :ntx], cells[0, :ntx, :], preferred_element_type=jnp.float32)
        rx = jnp.dot(hot[a:b, ntx:], cells[0, ntx : ntx + nrx, :], preferred_element_type=jnp.float32)
        sens[a:b, :] = (tx * rx * cond).astype(jnp.bfloat16)
        gram[a:b, :b] += lax.dot_general(
            sens[a:b, :], sens[:b, :], (ROWS_ROWS, ((), ())), preferred_element_type=jnp.float32
        )

    @pl.when(chunk == pl.num_programs(0) - 1)
    def _():
        finish(
            chosen_cols, cell_total, place, damping, order, trailing, factor,
            gram, high, low, column, work, upper,
        )


def finish(
    chosen_cols, cell_total, place, damping, order, trailing, factor, gram, high, low, column, work, upper
):
    rows = gram.shape[0]
    scale = 1.0 / cell_total
    row = lax.broadcasted_iota(jnp.int32, (BLOCK, BLOCK), 0)
    col = lax.broadcasted_iota(jnp.int32, (BLOCK, BLOCK), 1)
    for at in range(0, chosen_cols, BLOCK):
        end = at + BLOCK
        column[at:, :] = gram[at:, at:end] * scale
        column[at:end, :] += jnp.where(row == col, damping[:, at:end], 0.0)
        if at > 0:
            column[at:, :] -= product(
                (high[at:, :at], low[at:, :at]), (high[at:end, :at], low[at:end, :at]), ROWS_ROWS
            )
            high[:at, at:end] = jnp.zeros((at, BLOCK), jnp.bfloat16)
            low[:at, at:end] = jnp.zeros((at, BLOCK), jnp.bfloat16)
        factor_block(column[at:end, :], work, upper)
        h, l = halves(jnp.where(row >= col, upper[:, :BLOCK].T, 0.0))
        high[at:end, at:end] = h
        low[at:end, at:end] = l
        inverse = halves(upper[:, BLOCK:])
        h, l = halves(product(halves(column[end:, :]), inverse, ROWS_ROWS))
        high[end:, at:end] = h
        low[end:, at:end] = l

    group_rows, tile_cols = trailing.shape
    row_hot = (
        place[0] + lax.broadcasted_iota(jnp.int32, (group_rows, rows), 0) == order[...]
    ).astype(jnp.bfloat16)
    factor[...] = jnp.dot(row_hot, high[...], preferred_element_type=jnp.float32) + jnp.dot(
        row_hot, low[...], preferred_element_type=jnp.float32
    )
    left = rows - chosen_cols
    col_hot = (
        place[1] + lax.broadcasted_iota(jnp.int32, (tile_cols, left), 0) == order[:, chosen_cols:]
    ).astype(jnp.bfloat16)
    row_hot = row_hot[:, chosen_cols:]
    damp_left = damping[:, chosen_cols:]
    picked = []
    for a in range(0, left, BLOCK):
        b = min(a + BLOCK, left)
        at, end = chosen_cols + a, chosen_cols + b
        ids = lax.broadcasted_iota(jnp.int32, (left, b - a), 0)
        across = a + lax.broadcasted_iota(jnp.int32, (left, b - a), 1)
        lower = gram[chosen_cols:, at:end]
        strip = lower
        if a > 0:
            strip = jnp.concatenate([gram[at:end, chosen_cols:at].T, lower[a:]], axis=0)
        strip = strip * scale + jnp.where(ids == across, damp_left[:, a:b], 0.0)
        strip = strip - product(
            (high[chosen_cols:, :], low[chosen_cols:, :]), (high[at:end, :], low[at:end, :]), ROWS_ROWS
        )
        h, l = halves(strip)
        picked.append(
            jnp.dot(row_hot, h, preferred_element_type=jnp.float32)
            + jnp.dot(row_hot, l, preferred_element_type=jnp.float32)
        )
    h, l = halves(jnp.concatenate(picked, axis=1))
    trailing[...] = lax.dot_general(
        h, col_hot, (ROWS_ROWS, ((), ())), preferred_element_type=jnp.float32
    ) + lax.dot_general(l, col_hot, (ROWS_ROWS, ((), ())), preferred_element_type=jnp.float32)


def shards(
    tx_fields, rx_fields, layer_of_cell, layer_cond, tx_of_row, rx_of_row, damping, panel_order
):
    grp_count = lax.axis_size("grp")
    tile_count = lax.axis_size("tile")
    tile_cells = tx_fields.shape[1]
    ntx, nrx = tx_fields.shape[0], rx_fields.shape[0]
    rows = tx_of_row.shape[0]
    group_rows = rows // grp_count
    tile_cols = rows // tile_count
    grp, tile = lax.axis_index("grp"), lax.axis_index("tile")

    layers = jnp.broadcast_to(layer_of_cell.astype(jnp.bfloat16)[None, :], (PAD, tile_cells))
    own = jnp.concatenate([tx_fields, rx_fields, layers], axis=0)
    half = tile_cells // 2
    mine = lax.dynamic_slice_in_dim(own, (grp % 2) * half, half, axis=1)
    got = [
        lax.ppermute(mine, "tile", [(i, (i + k) % tile_count) for i in range(tile_count)])
        for k in range(1, tile_count)
    ]
    got = jnp.stack(got)
    other = lax.ppermute(got, "grp", [(i, i ^ 1) for i in range(grp_count)])
    cells = jnp.concatenate([jnp.stack([own[:, :half], own[:, half:]]), got, other], axis=0)

    tx_ids = jnp.take(tx_of_row, panel_order)
    rx_ids = jnp.take(rx_of_row, panel_order)
    damp = jnp.take(damping, panel_order)
    hot = jnp.concatenate(
        [
            tx_ids[:, None] == jnp.arange(ntx, dtype=jnp.int32)[None, :],
            rx_ids[:, None] == jnp.arange(nrx, dtype=jnp.int32)[None, :],
        ],
        axis=1,
    ).astype(jnp.bfloat16)
    place = jnp.stack([grp * group_rows, tile * tile_cols]).astype(jnp.int32)
    chosen_cols = PANEL * NPAN
    vmem = pl.BlockSpec(memory_space=pltpu.VMEM)
    call = pl.pallas_call(
        functools.partial(body, chosen_cols, tile_cells * tile_count),
        grid=(cells.shape[0],),
        in_specs=[
            pl.BlockSpec(memory_space=pltpu.SMEM),
            pl.BlockSpec((1,) + cells.shape[1:], lambda i: (i, 0, 0)),
            vmem, vmem, vmem, vmem,
        ],
        out_specs=[vmem, vmem],
        out_shape=[
            jax.ShapeDtypeStruct((group_rows, tile_cols), jnp.float32),
            jax.ShapeDtypeStruct((group_rows, chosen_cols), jnp.float32),
        ],
        scratch_shapes=[
            pltpu.VMEM((rows, rows), jnp.float32),
            pltpu.VMEM((rows, half), jnp.bfloat16),
            pltpu.VMEM((rows, chosen_cols), jnp.bfloat16),
            pltpu.VMEM((rows, chosen_cols), jnp.bfloat16),
            pltpu.VMEM((rows, BLOCK), jnp.float32),
            pltpu.VMEM((BLOCK, 2 * BLOCK), jnp.float32),
            pltpu.VMEM((BLOCK, 2 * BLOCK), jnp.float32),
        ],
        compiler_params=pltpu.CompilerParams(vmem_limit_bytes=60 * 2**20),
    )
    return tuple(
        call(
            place,
            cells,
            hot,
            jnp.broadcast_to(layer_cond[:, None], (layer_cond.shape[0], nrx)),
            damp[None, :],
            panel_order[None, :],
        )
    )


def solution(mesh):
    placed = (P(None, "tile"), P(None, "tile"), P("tile"), P(), P(), P(), P(), P())
    return jax.shard_map(
        shards,
        mesh=mesh,
        in_specs=placed,
        out_specs=(P("grp", "tile"), P("grp", None)),
        check_vma=False,
    )
```

time: 683 us -> 144 us (0.21)
  waiting for transfers between devices: 348 us -> 2.38 us
  other arithmetic: 243 us -> 4.91 us
  Pallas kernels: 0 us -> 85.6 us
  matrix products: 38.1 us -> 0 us
  between operations: 20.4 us -> 0.9 us
  starting transfers between devices: 0.59 us -> 13.9 us
  local copies, waits for them, and re-layouts: 27.9 us -> 35.5 us
    psum x4 -> x0, waiting for transfers between devices: 251 us -> none  [the longest x2 191 us: shards(): lax.psum((jnp.dot(trailing, col_pick, precision=highest), jnp.dot(panel_s...]
    another operation x35 -> x1, other arithmetic: 239 us -> 0.67 us  [shards(): place = jnp.stack([grp * group_rows, tile * tile_cols]).astype(jnp.int32)]
    pallas_call x0 -> x1, Pallas kernels: none -> 85.6 us  [shards(): call(place, cells, hot, jnp.broadcast_to(layer_cond[:, None], (layer_cond...]
    reduce_scatter x1 -> x0, waiting for transfers between devices: 67.5 us -> none  [shards(): lax.psum_scatter(lax.dot_general(lax.all_gather(sens_own, 'grp', axis=0,...]
    all_gather x1 -> x0, waiting for transfers between devices: 29.8 us -> none  [shards(): lax.all_gather(sens_own, 'grp', axis=0, tiled=True)]
    dot_general x10 -> x0, matrix products: 20.9 us -> none  [the longest x2 5.44 us: shards(): jnp.dot(panel_strip, col_pick, precision=highest)]
    gather x2 -> x3, local copies, waits for them, and re-layouts: 5.85 us -> 23.4 us  [the longest x1 7.78 us: shards(): damp = jnp.take(damping, panel_order)]
    another operation x40 -> x0, matrix products: 17.2 us -> none  [the longest x12 7.33 us: shards(): block_factor = jnp.linalg.cholesky(diag_block)]
  transfers between devices with their start and end apart: 6 -> 8, of which waited for: 6 -> 3; matrix products, arithmetic and copies ran while one was open for 1% -> 24% of each run, Pallas kernels for 0% -> 0%
where the time goes in v1:
time: 144 us; the launch traced here: 143 us
  Pallas kernels  85.6 us (59%)
  local copies, waits for them, and re-layouts  35.5 us (25%)
  starting transfers between devices  13.9 us (10%)
  other arithmetic  4.91 us (3%)
  waiting for transfers between devices  2.38 us (2%)
    pallas_call x1, Pallas kernels, shards(): call(place, cells, hot, jnp.broadcast_to(layer_cond[:, None], (layer_cond...  85.6 us
    ppermute x7, starting transfers between devices, shards(): lax.ppermute(mine, 'tile', [(i, (i + k) % tile_count) for i in range(tile...  13.8 us
    gather x1, local copies, waits for them, and re-layouts, shards(): damp = jnp.take(damping, panel_order)  7.78 us
    gather x1, local copies, waits for them, and re-layouts, shards(): tx_ids = jnp.take(tx_of_row, panel_order)  7.78 us
    gather x1, local copies, waits for them, and re-layouts, shards(): rx_ids = jnp.take(rx_of_row, panel_order)  7.78 us
    unnamed x22, local copies, waits for them, and re-layouts  6.74 us
  transfers between devices with their start and end apart: 8, of which 3 were waited for; matrix products, arithmetic and copies ran while one was open for 24% of the time, Pallas kernels for 0%

profile of v1, /device:TPU:0, one launch (start us, length us, event | category | flops | bytes accessed | tf_op | source)
XLA Modules:
  0.0 143.2 jit_solution(18384809669664911584)
XLA Ops:
  0.6 0.0 copy-start
  0.7 0.7 convert_element_type.6
  1.4 1.0 pad_maximum_fusion
  2.4 0.0 copy-start.4
  2.4 0.8 constant_dynamic-slice_fusion
  3.2 3.0 %collective-permute-start = (bf16[208,512]{1,0:T(8,128)(2,1)}, bf16[208,512]{1,0:T(8,128)(2,1)}, u32[]{:S(2)}, u32[]{:S(2)}) collective-permute-start(bf16[208,512]{1,0:T(8,128)(2,1)} %constant_dynamic-slice_fusion), channel_id=1, source_target_pairs={{0,1},{1,2},{2,3},{3,4},{4,5},{5,6},{6,7},{7,0},{8,9},{9,10},{10,1... | collective-permute-start | bytes 638984 | tf_op jit(solution)/shard_map/ppermute | solution.py:215
  6.1 1.6 %collective-permute-start.1 = (bf16[208,512]{1,0:T(8,128)(2,1)}, bf16[208,512]{1,0:T(8,128)(2,1)}, u32[]{:S(2)}, u32[]{:S(2)}) collective-permute-start(bf16[208,512]{1,0:T(8,128)(2,1)} %constant_dynamic-slice_fusion), channel_id=1, source_target_pairs={{0,2},{1,3},{2,4},{3,5},{4,6},{5,7},{6,0},{7,1},{8,10},{9,11},{10,... | collective-permute-start | bytes 638984 | tf_op jit(solution)/shard_map/ppermute | solution.py:215
  7.7 2.5 %collective-permute-start.2 = (bf16[208,512]{1,0:T(8,128)(2,1)}, bf16[208,512]{1,0:T(8,128)(2,1)}, u32[]{:S(2)}, u32[]{:S(2)}) collective-permute-start(bf16[208,512]{1,0:T(8,128)(2,1)} %constant_dynamic-slice_fusion), channel_id=1, source_target_pairs={{0,3},{1,4},{2,5},{3,6},{4,7},{5,0},{6,1},{7,2},{8,11},{9,12},{10,... | collective-permute-start | bytes 638984 | tf_op jit(solution)/shard_map/ppermute | solution.py:215
  10.2 1.2 collective-permute-start.3
  11.5 2.6 %collective-permute-start.4 = (bf16[208,512]{1,0:T(8,128)(2,1)}, bf16[208,512]{1,0:T(8,128)(2,1)}, u32[]{:S(2)}, u32[]{:S(2)}) collective-permute-start(bf16[208,512]{1,0:T(8,128)(2,1)} %constant_dynamic-slice_fusion), channel_id=1, source_target_pairs={{0,5},{1,6},{2,7},{3,0},{4,1},{5,2},{6,3},{7,4},{8,13},{9,14},{10,... | collective-permute-start | bytes 638984 | tf_op jit(solution)/shard_map/ppermute | solution.py:215
  14.1 0.0 copy-done.4
  14.1 0.7 compare_select_fusion
  14.8 1.3 broadcast_in_dim.38.order
  16.1 0.0 copy-done
  16.1 0.0 copy-start.5
  16.2 0.0 copy-start.1
  16.2 7.8 %gather_fusion = f32[1408]{0:T(1024)S(1)} fusion(f32[1408]{0:T(1024)S(1)} %copy-done, s32[2048]{0:T(1024)S(1)} %pad_clamp_fusion), kind=kCustom, calls=%fused_computation.2 | custom fusion | bytes 16896 | tf_op jit(solution)/shard_map/jit(_take)/gather | solution.py:224
  24.0 0.0 copy-done.5
  24.0 0.0 copy-done.1
  24.0 0.0 copy-start.2
  24.0 7.8 %gather_fusion.1 = s32[1408]{0:T(1024)S(1)} fusion(s32[1408]{0:T(1024)S(1)} %copy-done.1, s32[2048]{0:T(1024)S(1)} %pad_clamp_fusion), kind=kCustom, calls=%fused_computation.clone | custom fusion | bytes 16896 | tf_op jit(solution)/shard_map/jit(_take)/gather | solution.py:222
  31.8 0.0 copy-done.2
  31.8 7.8 %gather_fusion.2 = s32[1408]{0:T(1024)S(1)} fusion(s32[1408]{0:T(1024)S(1)} %copy-done.2, s32[2048]{0:T(1024)S(1)} %pad_clamp_fusion), kind=kCustom, calls=%fused_computation.1.clone | custom fusion | bytes 16896 | tf_op jit(solution)/shard_map/jit(_take)/gather | solution.py:223
  39.6 0.6 select_n.33.damping
  40.2 0.9 fusion
  41.2 0.0 collective-permute-done
  41.2 1.4 collective-permute-start.5
  42.6 1.0 bitcast_dynamic-update-slice_fusion.13
  43.5 0.0 collective-permute-done.1
  43.5 1.5 %collective-permute-start.6 = (bf16[208,512]{1,0:T(8,128)(2,1)}, bf16[208,512]{1,0:T(8,128)(2,1)S(1)}, u32[]{:S(2)}, u32[]{:S(2)}) collective-permute-start(bf16[208,512]{1,0:T(8,128)(2,1)} %constant_dynamic-slice_fusion), channel_id=1, source_target_pairs={{0,7},{1,0},{2,1},{3,2},{4,3},{5,4},{6,5},{7,6},{8,15},{9,8},{10,9... | collective-permute-start | bytes 638984 | tf_op jit(solution)/shard_map/ppermute | solution.py:215
  45.0 1.0 bitcast_dynamic-update-slice_fusion.11
  46.0 0.0 collective-permute-done.2
  46.0 1.0 bitcast_dynamic-update-slice_fusion.9
  46.9 0.0 collective-permute-done.3
  47.0 0.0 copy-start.6
  47.0 1.0 bitcast_dynamic-update-slice_fusion.7
  47.9 0.0 collective-permute-done.4
  48.0 1.0 bitcast_dynamic-update-slice_fusion.5
  48.9 0.4 collective-permute-done.5
  49.3 1.2 collective-permute-done.6
  50.6 0.1 collective-permute-start.7
  50.7 0.7 pad_add_fusion.place
  51.3 0.3 iota_compare_fusion
  51.6 0.3 iota_compare_fusion.1
  51.9 1.3 add_convert_fusion.hot
  53.2 0.8 collective-permute-done.7
  54.0 0.1 constant_dynamic-update-slice_fusion.cells
  54.1 0.0 copy-done.6
  54.1 0.0 copy-start.3
  54.1 0.8 broadcast_in_dim.21.layer_cond
  54.9 0.9 copy-done.3
  55.8 85.6 %shard_map.95 = (f32[352,176]{1,0:T(8,128)}, f32[352,1024]{1,0:T(8,128)}) custom-call(s32[2]{0:T(128)} %pad_add_fusion.place, bf16[16,208,512]{2,1,0:T(8,128)(2,1)} %copy-done.3, bf16[1408,192]{1,0:T(8,128)(2,1)} %add_convert_fusion.hot, f32[32,128]{1,0:T(8,128)} %broadcast_in_dim.21.layer_cond, f32[1,1408]{1,0:T(1,128)} %select_n.33.damping, ...), custom_call_target="tpu_custom_call" | custom-call | tf_op jit(solution)/shard_map/pallas_call | solution.py:260
  141.4 1.8 %copy.11 = f32[352,176]{0,1:T(8,128)} copy(f32[352,176]{1,0:T(8,128)} %get-tuple-element.5) | data formatting | bytes 495616 | tf_op jit(solution)/shard_map/pallas_call | solution.py:260
  (7 shorter events, 0.1 us)
Async XLA Ops:
  0.6 15.5 %copy-start = (f32[1408]{0:T(1024)S(1)}, f32[1408]{0:T(1024)}, u32[]{:S(2)}) copy-start(f32[1408]{0:T(1024)} %param.16) | copy-start | bytes 16900
  2.4 11.7 %copy-start.4 = (bf16[208,1024]{1,0:T(8,128)(2,1)}, bf16[208,1024]{1,0:T(8,128)(2,1)S(1)}, u32[]{:S(2)}) copy-start(bf16[208,1024]{1,0:T(8,128)(2,1)S(1)} %pad_maximum_fusion) | copy-start | bytes 1277956
  3.2 38.0 %collective-permute-start = (bf16[208,512]{1,0:T(8,128)(2,1)}, bf16[208,512]{1,0:T(8,128)(2,1)}, u32[]{:S(2)}, u32[]{:S(2)}) collective-permute-start(bf16[208,512]{1,0:T(8,128)(2,1)} %constant_dynamic-slice_fusion), channel_id=1, source_target_pairs={{0,1},{1,2},{2,3},{3,4},{4,5},{5,6},{6,7},{7,0},{8,9},{9,10},{10,1... | collective-permute-start | bytes 638984 | tf_op jit(solution)/shard_map/ppermute | solution.py:215
  6.1 37.4 %collective-permute-start.1 = (bf16[208,512]{1,0:T(8,128)(2,1)}, bf16[208,512]{1,0:T(8,128)(2,1)}, u32[]{:S(2)}, u32[]{:S(2)}) collective-permute-start(bf16[208,512]{1,0:T(8,128)(2,1)} %constant_dynamic-slice_fusion), channel_id=1, source_target_pairs={{0,2},{1,3},{2,4},{3,5},{4,6},{5,7},{6,0},{7,1},{8,10},{9,11},{10,... | collective-permute-start | bytes 638984 | tf_op jit(solution)/shard_map/ppermute | solution.py:215
  7.7 38.3 %collective-permute-start.2 = (bf16[208,512]{1,0:T(8,128)(2,1)}, bf16[208,512]{1,0:T(8,128)(2,1)}, u32[]{:S(2)}, u32[]{:S(2)}) collective-permute-start(bf16[208,512]{1,0:T(8,128)(2,1)} %constant_dynamic-slice_fusion), channel_id=1, source_target_pairs={{0,3},{1,4},{2,5},{3,6},{4,7},{5,0},{6,1},{7,2},{8,11},{9,12},{10,... | collective-permute-start | bytes 638984 | tf_op jit(solution)/shard_map/ppermute | solution.py:215
  10.2 36.7 %collective-permute-start.3 = (bf16[208,512]{1,0:T(8,128)(2,1)}, bf16[208,512]{1,0:T(8,128)(2,1)}, u32[]{:S(2)}, u32[]{:S(2)}) collective-permute-start(bf16[208,512]{1,0:T(8,128)(2,1)} %constant_dynamic-slice_fusion), channel_id=1, source_target_pairs={{0,4},{1,5},{2,6},{3,7},{4,0},{5,1},{6,2},{7,3},{8,12},{9,13},{10,... | collective-permute-start | bytes 638984 | tf_op jit(solution)/shard_map/ppermute | solution.py:215
  11.5 36.5 %collective-permute-start.4 = (bf16[208,512]{1,0:T(8,128)(2,1)}, bf16[208,512]{1,0:T(8,128)(2,1)}, u32[]{:S(2)}, u32[]{:S(2)}) collective-permute-start(bf16[208,512]{1,0:T(8,128)(2,1)} %constant_dynamic-slice_fusion), channel_id=1, source_target_pairs={{0,5},{1,6},{2,7},{3,0},{4,1},{5,2},{6,3},{7,4},{8,13},{9,14},{10,... | collective-permute-start | bytes 638984 | tf_op jit(solution)/shard_map/ppermute | solution.py:215
  16.1 7.8 %copy-start.5 = (s32[1408]{0:T(1024)S(1)}, s32[1408]{0:T(1024)}, u32[]{:S(2)}) copy-start(s32[1408]{0:T(1024)} %param.17) | copy-start | bytes 16900
  16.2 7.8 %copy-start.1 = (s32[1408]{0:T(1024)S(1)}, s32[1408]{0:T(1024)}, u32[]{:S(2)}) copy-start(s32[1408]{0:T(1024)} %param.14) | copy-start | bytes 16900
  24.0 7.8 %copy-start.2 = (s32[1408]{0:T(1024)S(1)}, s32[1408]{0:T(1024)}, u32[]{:S(2)}) copy-start(s32[1408]{0:T(1024)} %param.15) | copy-start | bytes 16900
  41.2 8.1 %collective-permute-start.5 = (bf16[208,512]{1,0:T(8,128)(2,1)}, bf16[208,512]{1,0:T(8,128)(2,1)S(1)}, u32[]{:S(2)}, u32[]{:S(2)}) collective-permute-start(bf16[208,512]{1,0:T(8,128)(2,1)} %constant_dynamic-slice_fusion), channel_id=1, source_target_pairs={{0,6},{1,7},{2,0},{3,1},{4,2},{5,3},{6,4},{7,5},{8,14},{9,15},{10,... | collective-permute-start | bytes 638984 | tf_op jit(solution)/shard_map/ppermute | solution.py:215
  43.5 7.0 %collective-permute-start.6 = (bf16[208,512]{1,0:T(8,128)(2,1)}, bf16[208,512]{1,0:T(8,128)(2,1)S(1)}, u32[]{:S(2)}, u32[]{:S(2)}) collective-permute-start(bf16[208,512]{1,0:T(8,128)(2,1)} %constant_dynamic-slice_fusion), channel_id=1, source_target_pairs={{0,7},{1,0},{2,1},{3,2},{4,3},{5,4},{6,5},{7,6},{8,15},{9,8},{10,9... | collective-permute-start | bytes 638984 | tf_op jit(solution)/shard_map/ppermute | solution.py:215
  47.0 7.1 %copy-start.6 = (f32[32]{0:T(128)S(1)}, f32[32]{0:T(128)}, u32[]{:S(2)}) copy-start(f32[32]{0:T(128)} %param.13) | copy-start | bytes 388
  50.6 3.4 %collective-permute-start.7 = (bf16[7,208,512]{2,1,0:T(8,128)(2,1)S(1)}, bf16[7,208,512]{2,1,0:T(8,128)(2,1)S(1)}, u32[]{:S(2)}, u32[]{:S(2)}) collective-permute-start(bf16[7,208,512]{2,1,0:T(8,128)(2,1)S(1)} %get-tuple-element.9), channel_id=1, source_target_pairs={{0,8},{8,0},{16,24},{24,16},{1,9},{9,1},{17,25},{25,17},{2,10},{10... | collective-permute-start | bytes 4472840 | tf_op jit(solution)/shard_map/ppermute | solution.py:219
  54.1 1.7 %copy-start.3 = (bf16[16,208,512]{2,1,0:T(8,128)(2,1)}, bf16[16,208,512]{2,1,0:T(8,128)(2,1)S(1)}, u32[]{:S(2)}) copy-start(bf16[16,208,512]{2,1,0:T(8,128)(2,1)S(1)} %constant_dynamic-update-slice_fusion.cells) | copy-start | bytes 10223620
